TPU v7x, 32 devices: a whole 2x2x4 slice. The times are simulated.
32 devices in a mesh: ctx: 4 (over x, core), head: 8 (over z, y).
Axes of the slice: x: 2, y: 2, z: 4, core: 2. Of those that a mesh axis runs over, the one named last changes fastest.
Arguments:
- q_nope: bfloat16 [512, 32, 128], P('ctx', 'head'), may hold values from -6 to 6
- q_rope: bfloat16 [512, 32, 64], P('ctx', 'head'), may hold values from -300 to 300
- w_uk: bfloat16 [32, 128, 512], P('head'), may hold values from -0.5 to 0.5
- w_uv: bfloat16 [32, 512, 128], P('head'), may hold values from -0.75 to 0.75
- w_o: bfloat16 [4096, 7168], P('head', 'ctx'), may hold values from -0.25 to 0.25
- cache_kv: bfloat16 [512, 576], P('ctx'), may hold values from -4 to 4
- new_kv: bfloat16 [512, 576], P('ctx'), may hold values from -4 to 4
- block_order: int32 [4], replicated, may hold values from 0 to 3, each once
- cache_lengths: int32 [4], replicated, may hold values from 32 to 128, as said below
Outputs:
- mixed: bfloat16 [512, 7168], P(('ctx', 'head'))
Inputs may be any that keep to these rules, and one draw needn't show every extreme that they name: `cache_lengths`: at least one ctx index has all 128 slots valid.
All inputs are finite; a program needn't handle non-finite values.
Results may differ from a plain program's by a relative error of at most 0.024.
Values may be sent and summed in bfloat16 or wider, within the bound.
A program may use at most 64 MiB of HBM per device.

v0:
```python
import jax
import jax.numpy as jnp
from jax import lax
from jax.sharding import PartitionSpec as P

neg_large = -1e30


def on_device(q_nope, q_rope, w_uk, w_uv, w_o, cache_kv, new_kv, block_order, cache_lengths):
    tok_rows, heads_here, nope_width = q_nope.shape
    latent_width = w_uk.shape[2]
    value_width = w_uv.shape[2]
    cache_rows = cache_kv.shape[0]
    shard_rows = cache_rows + tok_rows
    ctx_count = lax.axis_size("ctx")
    head_count = lax.axis_size("head")
    score_scale = float(nope_width + q_rope.shape[2]) ** (-0.5)
    query_rows = tok_rows * heads_here
    q_latent = jnp.einsum("thn,hnc->thc", q_nope, w_uk, preferred_element_type=jnp.float32)
    query = jnp.concatenate([q_latent, q_rope.astype(jnp.float32)], axis=2).astype(jnp.bfloat16)
    query = query.reshape(query_rows, query.shape[2])
    shard_ids = jnp.arange(ctx_count, dtype=jnp.int32)
    own_block = jnp.sum(jnp.where(shard_ids == lax.axis_index("ctx"), block_order, 0))
    query_pos = own_block * tok_rows + jnp.arange(query_rows, dtype=jnp.int32) // heads_here
    local_keys = jnp.concatenate([cache_kv, new_kv], axis=0)
    piece = lax.all_gather(local_keys, "ctx", axis=0, tiled=True)
    global_rows = jnp.arange(piece.shape[0], dtype=jnp.int32)
    owners = global_rows // shard_rows
    offsets = global_rows % shard_rows
    matches = owners[:, None] == shard_ids[None, :]
    lengths = jnp.sum(jnp.where(matches, cache_lengths[None, :], 0), axis=1)
    blocks = jnp.sum(jnp.where(matches, block_order[None, :], 0), axis=1)
    key_pos = blocks * tok_rows + offsets - cache_rows
    visible = jnp.where(
        (offsets < cache_rows)[None, :],
        (offsets < lengths)[None, :],
        key_pos[None, :] <= query_pos[:, None],
    )
    best = jnp.full((query_rows,), neg_large, jnp.float32)
    scores = (
        lax.dot_general(query, piece, (((1,), (1,)), ((), ())), preferred_element_type=jnp.float32)
        * score_scale
    )
    fresh = jnp.maximum(best, jnp.max(jnp.where(visible, scores, neg_large), axis=1))
    expo = jnp.where(visible, jnp.exp(scores - fresh[:, None]), 0.0)
    totals = jnp.sum(expo, axis=1)
    accum = jnp.dot(
        expo.astype(jnp.bfloat16), piece[:, :latent_width], preferred_element_type=jnp.float32
    )
    best, totals, accum = (fresh, totals, accum)
    latent_out = (
        (accum / totals[:, None]).astype(jnp.bfloat16).reshape(tok_rows, heads_here, latent_width)
    )
    head_out = jnp.einsum("thc,hcv->thv", latent_out, w_uv, preferred_element_type=jnp.float32)
    head_out = head_out.astype(jnp.bfloat16).reshape(tok_rows, heads_here * value_width)
    partial_rows = jnp.dot(
        lax.all_gather(head_out, "ctx", axis=0, tiled=True), w_o, preferred_element_type=jnp.float32
    )
    column_width = w_o.shape[1]
    own_rows = tok_rows // head_count
    grouped = partial_rows.reshape(ctx_count, head_count, own_rows, column_width)
    summed = lax.psum_scatter(grouped.astype(jnp.bfloat16), "head", scatter_dimension=1, tiled=True)
    regrouped = lax.all_to_all(summed, "ctx", split_axis=0, concat_axis=3, tiled=True)
    return regrouped.reshape(own_rows, ctx_count * column_width)


def solution(mesh):
    in_specs = (
        P("ctx", "head", None),
        P("ctx", "head", None),
        P("head", None, None),
        P("head", None, None),
        P("head", "ctx"),
        P("ctx", None),
        P("ctx", None),
        P(),
        P(),
    )
    out_specs = P(("ctx", "head"), None)
    return jax.shard_map(
        on_device, mesh=mesh, in_specs=in_specs, out_specs=out_specs, check_vma=False
    )
```

profile of v0, /device:TPU:1, one launch (start us, length us, event | category | flops | bytes accessed | tf_op | source)
XLA Modules:
  0.0 156.6 jit_solution(2597688266307848856)
XLA Ops:
  6.5 0.0 copy-start
  6.5 0.0 copy-start.2
  6.5 0.0 copy-start.4
  6.5 0.0 copy-start.3
  6.5 0.0 all-gather.2.cloned.1.call-start
  6.6 1.9 %pad_maximum_fusion = bf16[256,576]{0,1:T(8,128)(2,1)} fusion(bf16[128,576]{0,1:T(8,128)(2,1)} %param.15, bf16[128,576]{0,1:T(8,128)(2,1)} %param.14), kind=kLoop, calls=%fused_computation.24 | loop fusion | flops 589824 | bytes 589824 | tf_op jit(solution)/shard_map/concatenate | solution.py:25
  8.4 0.0 all-gather.2.cloned.1.call-update
  8.5 0.0 all-reduce.3.cloned.1.call-start
  8.5 1.4 fusion.3
  9.9 0.4 copy.32
  10.3 0.1 concatenate.12
  10.5 0.0 copy-done.2
  10.5 0.1 copy.33
  10.6 0.0 copy-done.4
  10.6 0.6 fusion.30
  12.0 0.0 copy-done.3
  12.0 0.1 select_reduce_fusion.2
  12.1 17.0 %all-gather.2.cloned.1.call-done = bf16[1024,576]{0,1:T(8,128)(2,1)} async-done(((bf16[256,576]{0,1:T(8,128)(2,1)}), bf16[1024,576]{0,1:T(8,128)(2,1)}) %all-gather.2.cloned.1.call-update) | async-done | bytes 1179664 | tf_op jit(solution)/shard_map/all_gather | solution.py:26
  29.0 2.5 %select_reduce_fusion = (f32[512]{0:T(512)S(1)}, f32[512,1024]{1,0:T(8,128)S(1)}) fusion(s32[1024]{0:T(1024)S(1)} %add_add_fusion, s32[512]{0:T(512)S(1)} %fusion.26, pred[1024]{0:T(1024)(128)(4,1)S(1)} %get-tuple-element.9, pred[1024]{0:T(1024)(128)(4,1)S(1)} %get-tuple-element.10, bf16[1024,576]{0,1:T(8,128)(2,1)} %all-gather.2.cloned.1.call-done, ...), kind=kOutput, calls=%fused_computation.2 | convolution fusion | flops 607780352 | bytes 3876864 | tf_op jit(solution)/shard_map/dot_general | solution.py:41
  31.6 0.0 copy-start.5
  31.6 0.9 fusion
  32.4 0.4 copy-done.5
  32.8 0.0 copy-start.1
  32.8 0.9 fusion.2
  33.7 0.1 reshape.72
  33.8 0.0 copy-done.1
  33.9 0.3 convolution_convert_fusion.2
  34.2 7.3 %all_gather.7 = bf16[512,512]{0,1:T(8,128)(2,1)S(1)} all-gather(bf16[128,512]{0,1:T(8,128)(2,1)S(1)} %bitcast.28), channel_id=1, replica_groups=mesh['ctx'=4,'head'=8] {'ctx'}, dimensions={0}, use_global_device_ids=true | all-gather | bytes 655360 | tf_op jit(solution)/shard_map/all_gather | solution.py:57
  41.6 0.0 copy-done
  41.6 0.0 copy-start.6
  41.6 2.4 %convolution_convert_fusion = bf16[512,1792]{1,0:T(8,128)(2,1)} fusion(bf16[512,512]{0,1:T(8,128)(2,1)S(1)} %all_gather.7, bf16[512,1792]{1,0:T(8,128)(2,1)S(1)} %copy-done), kind=kOutput, calls=%fused_computation | convolution fusion | flops 940441600 | bytes 4194304 | tf_op jit(solution)/shard_map/dot_general | solution.py:56
  43.9 0.0 all-reduce.3.cloned.1.call-update
  44.0 0.0 copy-done.6
  44.0 0.6 dynamic-slice
  44.6 95.1 %all-reduce.3.cloned.1.call-done = bf16[4,8,16,1792]{3,2,1,0:T(8,128)(2,1)} async-done(((bf16[4,8,16,1792]{3,2,1,0:T(8,128)(2,1)}), bf16[4,8,16,1792]{3,2,1,0:T(8,128)(2,1)}) %all-reduce.3.cloned.1.call-update) | async-done | bytes 1835024
  139.6 1.6 %constant_dynamic-slice_fusion = bf16[4,1,16,1792]{3,2,1,0:T(8,128)(2,1)S(1)} fusion(bf16[4,8,16,1792]{3,2,1,0:T(8,128)(2,1)} %all-reduce.3.cloned.1.call-done, u32[]{:T(128)} %bitcast.14), kind=kLoop, calls=%fused_computation.53 | loop fusion | bytes 458756
  141.2 7.7 %all_to_all.15 = bf16[4,1,16,1792]{3,2,1,0:T(8,128)(2,1)S(1)} all-to-all(bf16[4,1,16,1792]{3,2,1,0:T(8,128)(2,1)S(1)} %constant_dynamic-slice_fusion), channel_id=1, replica_groups=mesh['ctx'=4,'head'=8] {'ctx'}, dimensions={0} | all-to-all | bytes 458752 | tf_op jit(solution)/shard_map/all_to_all | solution.py:63
  148.9 0.1 copy.36
  149.1 0.7 copy.40
  (5 shorter events, 0.0 us)
Async XLA Ops:
  6.5 35.0 %copy-start = (bf16[512,1792]{1,0:T(8,128)(2,1)S(1)}, bf16[512,1792]{1,0:T(8,128)(2,1)}, u32[]{:S(2)}) copy-start(bf16[512,1792]{1,0:T(8,128)(2,1)} %param.13) | copy-start | bytes 5505028
  6.5 3.9 %copy-start.2 = (bf16[128,4,64]{0,2,1:T(8,128)(2,1)S(1)}, bf16[128,4,64]{0,2,1:T(8,128)(2,1)}, u32[]{:S(2)}) copy-start(bf16[128,4,64]{0,2,1:T(8,128)(2,1)} %param.10) | copy-start | bytes 196612
  6.5 4.1 %copy-start.4 = (s32[4]{0:T(128)S(1)}, s32[4]{0:T(128)}, u32[]{:S(2)}) copy-start(s32[4]{0:T(128)} %param.16) | copy-start | bytes 52
  6.5 5.4 %copy-start.3 = (s32[4]{0:T(128)S(1)}, s32[4]{0:T(128)}, u32[]{:S(2)}) copy-start(s32[4]{0:T(128)} %param.17) | copy-start | bytes 52
  6.5 22.5 %all-gather.2.cloned.1.call-start = ((), (), s32[]{:S(2)}) async-start(), calls=%async_computation.1 | async-start | bytes 1474560 | tf_op jit(solution)/shard_map/all_gather | solution.py:26
  8.5 131.1 %all-reduce.3.cloned.1.call-start = ((), (), s32[]{:S(2)}) async-start(), calls=%async_computation.2 | async-start | bytes 3670016
  31.6 1.3 copy-start.5
  32.8 1.0 copy-start.1
  41.6 2.4 %copy-start.6 = (u32[32]{0:T(128)S(1)}, u32[32]{0:T(128)}, u32[]{:S(2)}) copy-start(u32[32]{0:T(128)} %constant.72) | copy-start | bytes 388
Sparse Core Ops, SparseCore 0:
  8.9 20.0 all-gather.1
  44.1 95.4 all-reduce.2
where the time goes:
time: 158 us; the launch traced here: 157 us
  waiting for transfers between devices  112 us (71%)
  blocking collectives  15.1 us (10%)
  between operations  14.2 us (9%)
  matrix products  7.5 us (5%)
  local copies, waits for them, and re-layouts  4.25 us (3%)
  other arithmetic  3.49 us (2%)
    unnamed x3, waiting for transfers between devices  95.1 us
    all_gather x1, waiting for transfers between devices, on_device(): piece = lax.all_gather(local_keys, 'ctx', axis=0, tiled=True)  17 us
    all_to_all x1, blocking collectives, on_device(): lax.all_to_all(summed, 'ctx', split_axis=0, concat_axis=3, tiled=True)  7.73 us
    all_gather x1, blocking collectives, on_device(): lax.all_gather(head_out, 'ctx', axis=0, tiled=True)  7.33 us
    unnamed x18, local copies, waits for them, and re-layouts  3.47 us
  transfers between devices with their start and end apart: 2, of which 2 were waited for; matrix products, arithmetic and copies ran while one was open for 2% of the time, Pallas kernels for 0%

commit v1 on v0

--- a/solution.py
+++ b/solution.py
@@ -1,12 +1,17 @@
+import functools
+
 import jax
 import jax.numpy as jnp
 from jax import lax
+from jax.experimental import pallas as pl
+from jax.experimental.pallas import tpu as pltpu
 from jax.sharding import PartitionSpec as P
 
 neg_large = -1e30
-
-
-def on_device(q_nope, q_rope, w_uk, w_uv, w_o, cache_kv, new_kv, block_order, cache_lengths):
+MESH = pl.DeviceIdType.MESH
+
+
+def plain_on_device(q_nope, q_rope, w_uk, w_uv, w_o, cache_kv, new_kv, block_order, cache_lengths):
     tok_rows, heads_here, nope_width = q_nope.shape
     latent_width = w_uk.shape[2]
     value_width = w_uv.shape[2]
@@ -64,6 +69,327 @@
     return regrouped.reshape(own_rows, ctx_count * column_width)
 
 
+def flip(index, bit):
+    return index + bit - 2 * bit * lax.rem(lax.div(index, bit), 2)
+
+
+def flip_all(index, mask):
+    bit = 1
+    while bit <= mask:
+        if mask & bit:
+            index = flip(index, bit)
+        bit *= 2
+    return index
+
+
+def bits_of(count):
+    return [1 << k for k in range(count.bit_length() - 1)]
+
+
+def low_bit(mask):
+    return mask & -mask
+
+
+def column_groups(width, head_bits):
+    if len(head_bits) < 2:
+        return [(0, width, tuple(head_bits))]
+    first = (width * 5 // 7) // 128 * 128
+    swapped = (head_bits[1], head_bits[0]) + tuple(head_bits[2:])
+    return [(0, first, tuple(head_bits)), (first, width - first, swapped)]
+
+
+def kernel(dims, qn_ref, qr_ref, uk_ref, uv_hbm, wo_hbm, ck_ref, nk_ref, order_ref, lens_ref, out_ref, *scratch):
+    n_ctx, n_head, tok, heads, nope, rope, latent, vdim, slots, groups = dims
+    n_groups = len(groups)
+    query, kv, acc, ho, uv_ref, wo_ref = scratch[:6]
+    snd = scratch[6 : 6 + n_groups]
+    rcv = scratch[6 + n_groups : 6 + 2 * n_groups]
+    tot = scratch[6 + 2 * n_groups : 6 + 3 * n_groups]
+    loc_sem, kv_ssem, kv_rsem, ho_ssem, ho_rsem, rs_ssem, rs_rsem, out_ssem, out_rsem = scratch[6 + 3 * n_groups :]
+    ctx, hd = lax.axis_index("ctx"), lax.axis_index("head")
+    ctx_bits, head_bits = bits_of(n_ctx), bits_of(n_head)
+    nb = len(head_bits)
+    own = tok // n_head
+    keys = slots + tok
+    rows = heads * tok
+    f32, bf16 = jnp.float32, jnp.bfloat16
+
+    def peer(ctx_mask=0, head_bit=0):
+        return {
+            "ctx": flip_all(ctx, ctx_mask),
+            "head": flip(hd, head_bit) if head_bit else hd,
+        }
+
+    local = [
+        pltpu.make_async_copy(ck_ref, kv.at[0, :, 0:slots], loc_sem.at[0]),
+        pltpu.make_async_copy(nk_ref, kv.at[0, :, slots:keys], loc_sem.at[1]),
+        pltpu.make_async_copy(uv_hbm, uv_ref, loc_sem.at[2]),
+        pltpu.make_async_copy(wo_hbm, wo_ref, loc_sem.at[3]),
+    ]
+    for copy in local:
+        copy.start()
+
+    barrier = pltpu.get_barrier_semaphore()
+    for mask in range(1, n_ctx):
+        pl.semaphore_signal(barrier, inc=1, device_id=peer(mask), device_id_type=MESH)
+    for bit in head_bits:
+        pl.semaphore_signal(barrier, inc=1, device_id=peer(0, bit), device_id_type=MESH)
+    pl.semaphore_wait(barrier, n_ctx - 1 + nb)
+
+    sends = []
+
+    def send(src, dst, ssem, rsem, device):
+        copy = pltpu.make_async_remote_copy(
+            src_ref=src, dst_ref=dst, send_sem=ssem, recv_sem=rsem, device_id=device, device_id_type=MESH
+        )
+        copy.start()
+        sends.append(copy)
+        return copy
+
+    kv_in = {}
+    spans = [(0, slots), (slots, keys)]
+
+    def pass_keys(mask, part):
+        lo, hi = spans[part]
+        for bit in reversed(ctx_bits):
+            if mask == 0 or bit < low_bit(mask):
+                src = (ck_ref, nk_ref)[part] if mask == 0 else kv.at[mask, :, lo:hi]
+                kv_in[mask | bit, part] = send(
+                    src,
+                    kv.at[mask | bit, :, lo:hi],
+                    kv_ssem.at[mask | bit, part],
+                    kv_rsem.at[mask | bit, part],
+                    peer(bit),
+                )
+
+    for part in range(2):
+        pass_keys(0, part)
+
+    order0 = groups[0][2]
+    place = lax.broadcasted_iota(jnp.int32, (tok, 1), 0)
+    block = place // own
+    token = place % own
+    for at, bit in enumerate(order0):
+        digit = (block // (1 << (nb - 1 - at))) % 2
+        mine = lax.rem(lax.div(hd, bit), 2)
+        token = token + own * bit * (digit + mine - 2 * digit * mine)
+    flat = lax.broadcasted_iota(jnp.int32, (tok, rows), 1)
+    pick = (lax.broadcasted_iota(jnp.int32, (tok, tok), 1) == token).astype(bf16)
+    q_all = qn_ref[...]
+    for h in range(heads):
+        choose = (flat == token * heads + h).astype(bf16)
+        q_h = jnp.dot(choose, q_all, preferred_element_type=f32).astype(bf16)
+        lat = jnp.dot(q_h, uk_ref[h], preferred_element_type=f32)
+        span = slice(h * tok, (h + 1) * tok)
+        query[span, 0:latent] = lat.astype(bf16)
+        turned = lax.dot_general(pick, qr_ref[h], (((1,), (1,)), ((), ())), preferred_element_type=f32)
+        query[span, latent : latent + rope] = turned.astype(bf16)
+
+    scale = float(nope + rope) ** (-0.5)
+    q_pos = order_ref[ctx] * tok + jnp.concatenate([token] * heads, axis=0)
+    col = lax.broadcasted_iota(jnp.int32, (rows, keys), 1)
+
+    best = total = None
+    for mask in range(n_ctx):
+        for part in range(2):
+            if mask == 0:
+                local[part].wait()
+            else:
+                kv_in[mask, part].wait_recv()
+                pass_keys(mask, part)
+        source = flip_all(ctx, mask)
+        length = lens_ref[source]
+        key_pos = col - slots + order_ref[source] * tok
+        seen = jnp.where(col < slots, col - length + 1, key_pos - q_pos) <= 0
+        s = jnp.dot(query[...], kv[mask], preferred_element_type=f32) * scale
+        s = jnp.where(seen, s, neg_large)
+        top = jnp.max(s, axis=1, keepdims=True)
+        if mask:
+            top = jnp.maximum(best, top)
+        e = jnp.exp(s - top)
+        part_sum = jnp.sum(e, axis=1, keepdims=True)
+        mixed = lax.dot_general(
+            e.astype(bf16), kv[mask, 0:latent, :], (((1,), (1,)), ((), ())), preferred_element_type=f32
+        )
+        if mask:
+            shrink = jnp.exp(best - top)
+            total = total * shrink + part_sum
+            mixed = acc[...] * shrink + mixed
+        else:
+            total = part_sum
+        best = top
+        if mask < n_ctx - 1:
+            acc[...] = mixed
+
+    lat_out = (mixed / total).astype(bf16)
+    local[2].wait()
+    for h in range(heads):
+        ho[0, :, h * vdim : (h + 1) * vdim] = jnp.dot(
+            lat_out[h * tok : (h + 1) * tok], uv_ref[h], preferred_element_type=f32
+        ).astype(bf16)
+    ho_in = {}
+
+    def pass_heads(mask):
+        for bit in reversed(ctx_bits):
+            if mask == 0 or bit < low_bit(mask):
+                ho_in[mask | bit] = send(
+                    ho.at[mask], ho.at[mask | bit], ho_ssem.at[mask | bit], ho_rsem.at[mask | bit], peer(bit)
+                )
+
+    pass_heads(0)
+    local[3].wait()
+
+    items = [(mask, g) for mask in range(n_ctx) for g in range(n_groups)]
+    moving = {}
+
+    def push(at, step):
+        mask, g = items[at]
+        size = tok >> (step + 1)
+        moving[at, step] = send(
+            snd[g].at[mask, size : 2 * size],
+            rcv[g].at[mask, size : 2 * size],
+            rs_ssem.at[at, step],
+            rs_rsem.at[at, step],
+            peer(0, groups[g][2][step]),
+        )
+
+    def first_step(at):
+        mask, g = items[at]
+        lo, width, order = groups[g]
+        x = ho[mask]
+        if order != order0:
+            def at_block(p):
+                m = sum(order[k] for k in range(nb) if p >> (nb - 1 - k) & 1)
+                return sum(1 << (nb - 1 - k) for k in range(nb) if m & order0[k])
+
+            x = jnp.concatenate([x[at_block(p) * own : (at_block(p) + 1) * own] for p in range(n_head)], axis=0)
+        y = jnp.dot(x, wo_ref[:, lo : lo + width], preferred_element_type=f32)
+        tot[g][mask] = y[0 : tok // 2]
+        snd[g][mask, tok // 2 : tok] = y[tok // 2 :].astype(bf16)
+        push(at, 0)
+
+    def later_step(at, step):
+        mask, g = items[at]
+        lo, width, order = groups[g]
+        size = tok >> step
+        moving[at, step - 1].wait_recv()
+        y = tot[g][mask, 0:size] + rcv[g][mask, size : 2 * size].astype(f32)
+        if step < nb:
+            half = size // 2
+            snd[g][mask, half:size] = y[half:].astype(bf16)
+            tot[g][mask, 0:half] = y[:half]
+            push(at, step)
+        elif mask == 0:
+            out_ref[ctx, :, lo : lo + width] = y.astype(bf16)
+        else:
+            snd[g][mask, 0:own] = y.astype(bf16)
+            send(
+                snd[g].at[mask, 0:own],
+                out_ref.at[ctx, :, lo : lo + width],
+                out_ssem.at[at],
+                out_rsem.at[at],
+                peer(mask),
+            )
+
+    for at, (mask, g) in enumerate(items):
+        if mask and g == 0:
+            ho_in[mask].wait_recv()
+            pass_heads(mask)
+        first_step(at)
+    lag = n_groups
+    for key in range(len(items) + lag * (nb - 1)):
+        for step in range(1, nb + 1):
+            at = key - lag * (step - 1)
+            if 0 <= at < len(items):
+                later_step(at, step)
+
+    for at, (mask, g) in enumerate(items):
+        if mask:
+            lo, width, order = groups[g]
+            pltpu.make_async_remote_copy(
+                src_ref=snd[g].at[mask, 0:own],
+                dst_ref=out_ref.at[flip_all(ctx, mask), :, lo : lo + width],
+                send_sem=out_ssem.at[at],
+                recv_sem=out_rsem.at[at],
+                device_id=peer(mask),
+                device_id_type=MESH,
+            ).wait_recv()
+    for copy in sends:
+        copy.wait_send()
+
+
+def on_device(q_nope, q_rope, w_uk, w_uv, w_o, cache_kv, new_kv, block_order, cache_lengths):
+    tok, heads, nope = q_nope.shape
+    rope = q_rope.shape[2]
+    latent, vdim = w_uk.shape[2], w_uv.shape[2]
+    slots = cache_kv.shape[0]
+    depth, width = w_o.shape
+    n_ctx, n_head = lax.axis_size("ctx"), lax.axis_size("head")
+    own = tok // n_head
+    full = (
+        own % 16 == 0
+        and width % 256 == 0
+        and slots % 128 == 0
+        and tok % 128 == 0
+        and n_ctx & (n_ctx - 1) == 0
+        and n_head & (n_head - 1) == 0
+        and n_head > 1
+    )
+    if not full:
+        return plain_on_device(q_nope, q_rope, w_uk, w_uv, w_o, cache_kv, new_kv, block_order, cache_lengths)
+    groups = tuple(column_groups(width, bits_of(n_head)))
+    nb = len(bits_of(n_head))
+    dims = (n_ctx, n_head, tok, heads, nope, rope, latent, vdim, slots, groups)
+    bf16, f32 = jnp.bfloat16, jnp.float32
+    n_items = n_ctx * len(groups)
+    dma = pltpu.SemaphoreType.DMA
+    vmem = pl.BlockSpec(memory_space=pltpu.VMEM)
+    smem = pl.BlockSpec(memory_space=pltpu.SMEM)
+    anywhere = pl.BlockSpec(memory_space=pl.ANY)
+    scratch = [
+        pltpu.VMEM((heads * tok, latent + rope), bf16),
+        pltpu.VMEM((n_ctx, latent + rope, slots + tok), bf16),
+        pltpu.VMEM((heads * tok, latent), f32),
+        pltpu.VMEM((n_ctx, tok, heads * vdim), bf16),
+        pltpu.VMEM(w_uv.shape, bf16),
+        pltpu.VMEM(w_o.shape, bf16),
+    ]
+    scratch += [pltpu.VMEM((n_ctx, tok, g[1]), bf16) for g in groups] * 2
+    scratch += [pltpu.VMEM((n_ctx, tok // 2, g[1]), f32) for g in groups]
+    scratch += [
+        dma((4,)),
+        dma((n_ctx, 2)),
+        dma((n_ctx, 2)),
+        dma((n_ctx,)),
+        dma((n_ctx,)),
+        dma((n_items, nb)),
+        dma((n_items, nb)),
+        dma((n_items,)),
+        dma((n_items,)),
+    ]
+    out = pl.pallas_call(
+        functools.partial(kernel, dims),
+        out_shape=jax.ShapeDtypeStruct((n_ctx, own, width), bf16),
+        in_specs=[vmem, vmem, vmem, anywhere, anywhere, anywhere, anywhere, smem, smem],
+        out_specs=vmem,
+        scratch_shapes=scratch,
+        compiler_params=pltpu.CompilerParams(
+            collective_id=0, has_side_effects=True, vmem_limit_bytes=60 * 1024 * 1024
+        ),
+    )(
+        q_nope.reshape(tok * heads, nope),
+        q_rope.transpose(1, 2, 0),
+        w_uk,
+        w_uv,
+        w_o,
+        cache_kv.T,
+        new_kv.T,
+        block_order,
+        cache_lengths,
+    )
+    return out.transpose(1, 0, 2).reshape(own, n_ctx * width)
+
+
 def solution(mesh):
     in_specs = (
         P("ctx", "head", None),

time: 158 us -> 51.7 us (0.33)
  waiting for transfers between devices: 112 us -> 0 us
  Pallas kernels: 0 us -> 49.9 us
  blocking collectives: 15.1 us -> 0 us
  between operations: 14.2 us -> 0.01 us
  matrix products: 7.5 us -> 0 us
  other arithmetic: 3.49 us -> 0 us
  local copies, waits for them, and re-layouts: 4.25 us -> 1.64 us
    unnamed x3 -> x0, waiting for transfers between devices: 95.1 us -> none
    pallas_call x0 -> x1, Pallas kernels: none -> 49.9 us  [on_device(): pl.pallas_call(functools.partial(kernel, dims), out_shape=jax.ShapeDtypeS...]
    all_gather x1 -> x0, waiting for transfers between devices: 17 us -> none  [on_device(): piece = lax.all_gather(local_keys, 'ctx', axis=0, tiled=True)]
    all_to_all x1 -> x0, blocking collectives: 7.73 us -> none  [on_device(): lax.all_to_all(summed, 'ctx', split_axis=0, concat_axis=3, tiled=True)]
    dot_general x5 -> x0, matrix products: 7.5 us -> none  [the longest x1 2.51 us: on_device(): lax.dot_general(query, piece, (((1,), (1,)), ((), ())), preferred_element...]
    all_gather x1 -> x0, blocking collectives: 7.33 us -> none  [on_device(): lax.all_gather(head_out, 'ctx', axis=0, tiled=True)]
    unnamed x18 -> x0, local copies, waits for them, and re-layouts: 3.47 us -> none
    concatenate x1 -> x0, other arithmetic: 1.86 us -> none  [on_device(): local_keys = jnp.concatenate([cache_kv, new_kv], axis=0)]
  transfers between devices with their start and end apart: 2 -> 0, of which waited for: 2 -> 0; matrix products, arithmetic and copies ran while one was open for 2% -> 0% of each run, Pallas kernels for 0% -> 0%
where the time goes in v1:
time: 51.7 us; the launch traced here: 51.5 us
  Pallas kernels  49.9 us (97%)
  local copies, waits for them, and re-layouts  1.64 us (3%)
    pallas_call x1, Pallas kernels, on_device(): pl.pallas_call(functools.partial(kernel, dims), out_shape=jax.ShapeDtypeS...  49.9 us
    reshape x1, local copies, waits for them, and re-layouts, on_device(): return out.transpose(1, 0, 2).reshape(own, n_ctx * width)  1.64 us

profile of v1, /device:TPU:1, one launch (start us, length us, event | category | flops | bytes accessed | tf_op | source)
XLA Modules:
  0.0 51.5 jit_solution(3258498572779147883)
XLA Ops:
  0.0 49.9 %shard_map.91 = bf16[4,16,1792]{2,1,0:T(8,128)(2,1)} custom-call(bf16[512,128]{1,0:T(8,128)(2,1)} %bitcast.10, bf16[4,64,128]{2,1,0:T(8,128)(2,1)} %bitcast.11, bf16[4,128,512]{2,1,0:T(8,128)(2,1)} %uk_ref.1, bf16[4,512,128]{2,1,0:T(8,128)(2,1)} %uv_hbm.1, bf16[512,1792]{1,0:T(8,128)(2,1)} %wo_hbm.1, bf16[576,128]{1,0:T(8,128)(2,1)} %bitcast.8, ...), custom_call_target="tpu_custom_call" | custom-call | tf_op jit(solution)/shard_map/pallas_call | solution.py:370
  49.9 1.6 %copy.11 = bf16[4,2,8,1792]{3,2,0,1:T(8,128)(2,1)} copy(bf16[4,2,8,1792]{3,2,1,0:T(8,128)(2,1)} %bitcast.7) | data formatting | bytes 458752 | tf_op jit(solution)/shard_map/reshape | solution.py:390

commit v2 on v1

--- a/solution.py
+++ b/solution.py
@@ -91,25 +91,31 @@
 
 
 def column_groups(width, head_bits):
-    if len(head_bits) < 2:
-        return [(0, width, tuple(head_bits))]
-    first = (width * 5 // 7) // 128 * 128
-    swapped = (head_bits[1], head_bits[0]) + tuple(head_bits[2:])
-    return [(0, first, tuple(head_bits)), (first, width - first, swapped)]
+    first = (width * 4 // 7) // 256 * 256
+    near, far = head_bits[0], head_bits[1]
+    return (
+        (0, first // 2, near, tuple(b for b in head_bits if b != near)),
+        (first, (width - first) // 2, far, tuple(b for b in head_bits if b != far)),
+    )
 
 
 def kernel(dims, qn_ref, qr_ref, uk_ref, uv_hbm, wo_hbm, ck_ref, nk_ref, order_ref, lens_ref, out_ref, *scratch):
     n_ctx, n_head, tok, heads, nope, rope, latent, vdim, slots, groups = dims
     n_groups = len(groups)
-    query, kv, acc, ho, uv_ref, wo_ref = scratch[:6]
-    snd = scratch[6 : 6 + n_groups]
-    rcv = scratch[6 + n_groups : 6 + 2 * n_groups]
-    tot = scratch[6 + 2 * n_groups : 6 + 3 * n_groups]
-    loc_sem, kv_ssem, kv_rsem, ho_ssem, ho_rsem, rs_ssem, rs_rsem, out_ssem, out_rsem = scratch[6 + 3 * n_groups :]
+    query, kv, acc, ho, hx, uv_ref = scratch[:6]
+    wide = scratch[6 : 6 + n_groups]
+    snd = scratch[6 + n_groups : 6 + 2 * n_groups]
+    rcv = scratch[6 + 2 * n_groups : 6 + 3 * n_groups]
+    tot = scratch[6 + 3 * n_groups : 6 + 4 * n_groups]
+    sems = scratch[6 + 4 * n_groups :]
+    loc_sem, kv_ssem, kv_rsem, ho_ssem, ho_rsem, hx_ssem, hx_rsem, w_ssem, w_rsem = sems[:9]
+    rs_ssem, rs_rsem, out_ssem, out_rsem = sems[9:]
     ctx, hd = lax.axis_index("ctx"), lax.axis_index("head")
     ctx_bits, head_bits = bits_of(n_ctx), bits_of(n_head)
     nb = len(head_bits)
+    n_steps = nb - 1
     own = tok // n_head
+    depth = heads * vdim
     keys = slots + tok
     rows = heads * tok
     f32, bf16 = jnp.float32, jnp.bfloat16
@@ -124,17 +130,29 @@
         pltpu.make_async_copy(ck_ref, kv.at[0, :, 0:slots], loc_sem.at[0]),
         pltpu.make_async_copy(nk_ref, kv.at[0, :, slots:keys], loc_sem.at[1]),
         pltpu.make_async_copy(uv_hbm, uv_ref, loc_sem.at[2]),
-        pltpu.make_async_copy(wo_hbm, wo_ref, loc_sem.at[3]),
     ]
+
+    def kept(g, swapped=False):
+        lo, width, bit, _ = groups[g]
+        upper = lax.rem(lax.div(hd, bit), 2)
+        upper = 1 - upper if swapped else upper
+        return pl.ds(pl.multiple_of(lo + width * upper, 128), width)
+
+    for g in range(n_groups):
+        local.append(
+            pltpu.make_async_copy(wo_hbm.at[:, kept(g)], wide[g].at[0:depth], loc_sem.at[3 + g])
+        )
     for copy in local:
         copy.start()
 
     barrier = pltpu.get_barrier_semaphore()
     for mask in range(1, n_ctx):
         pl.semaphore_signal(barrier, inc=1, device_id=peer(mask), device_id_type=MESH)
+    swaps = [group[2] for group in groups]
     for bit in head_bits:
-        pl.semaphore_signal(barrier, inc=1, device_id=peer(0, bit), device_id_type=MESH)
-    pl.semaphore_wait(barrier, n_ctx - 1 + nb)
+        for mask in range(n_ctx if bit in swaps else 1):
+            pl.semaphore_signal(barrier, inc=1, device_id=peer(mask, bit), device_id_type=MESH)
+    pl.semaphore_wait(barrier, n_ctx - 1 + nb + (n_ctx - 1) * len(swaps))
 
     sends = []
 
@@ -165,7 +183,18 @@
     for part in range(2):
         pass_keys(0, part)
 
-    order0 = groups[0][2]
+    w_in = [
+        send(
+            wo_hbm.at[:, kept(g, True)],
+            wide[g].at[depth : 2 * depth],
+            w_ssem.at[g],
+            w_rsem.at[g],
+            peer(0, groups[g][2]),
+        )
+        for g in range(n_groups)
+    ]
+
+    order0 = tuple(head_bits)
     place = lax.broadcasted_iota(jnp.int32, (tok, 1), 0)
     block = place // own
     token = place % own
@@ -227,7 +256,12 @@
         ho[0, :, h * vdim : (h + 1) * vdim] = jnp.dot(
             lat_out[h * tok : (h + 1) * tok], uv_ref[h], preferred_element_type=f32
         ).astype(bf16)
-    ho_in = {}
+    ho_in, hx_in = {}, {}
+
+    def pass_partner(g, mask, src):
+        hx_in[g, mask] = send(
+            src, hx.at[g, mask], hx_ssem.at[g, mask], hx_rsem.at[g, mask], peer(0, groups[g][2])
+        )
 
     def pass_heads(mask):
         for bit in reversed(ctx_bits):
@@ -235,9 +269,21 @@
                 ho_in[mask | bit] = send(
                     ho.at[mask], ho.at[mask | bit], ho_ssem.at[mask | bit], ho_rsem.at[mask | bit], peer(bit)
                 )
+        if mask % 2 == 0:
+            for g in range(n_groups):
+                pass_partner(g, mask, ho.at[mask])
+
+    def pass_across(g, mask):
+        if mask % 2 == 0:
+            hx_in[g, mask + 1] = send(
+                hx.at[g, mask],
+                hx.at[g, mask + 1],
+                hx_ssem.at[g, mask + 1],
+                hx_rsem.at[g, mask + 1],
+                peer(1),
+            )
 
     pass_heads(0)
-    local[3].wait()
 
     items = [(mask, g) for mask in range(n_ctx) for g in range(n_groups)]
     moving = {}
@@ -250,70 +296,86 @@
             rcv[g].at[mask, size : 2 * size],
             rs_ssem.at[at, step],
             rs_rsem.at[at, step],
-            peer(0, groups[g][2][step]),
-        )
+            peer(0, groups[g][3][step]),
+        )
+
+    def at_block(p, order, other):
+        m = sum(order[k] for k in range(nb) if p >> (nb - 1 - k) & 1) ^ other
+        return sum(1 << (nb - 1 - k) for k in range(nb) if m & order0[k])
+
+    def placed(x, order, other):
+        spots = [at_block(p, order, other) for p in range(n_head)]
+        return jnp.concatenate([x[k * own : (k + 1) * own] for k in spots], axis=0)
 
     def first_step(at):
         mask, g = items[at]
-        lo, width, order = groups[g]
-        x = ho[mask]
-        if order != order0:
-            def at_block(p):
-                m = sum(order[k] for k in range(nb) if p >> (nb - 1 - k) & 1)
-                return sum(1 << (nb - 1 - k) for k in range(nb) if m & order0[k])
-
-            x = jnp.concatenate([x[at_block(p) * own : (at_block(p) + 1) * own] for p in range(n_head)], axis=0)
-        y = jnp.dot(x, wo_ref[:, lo : lo + width], preferred_element_type=f32)
+        lo, width, bit, steps = groups[g]
+        order = steps + (bit,)
+        x = jnp.concatenate([placed(ho[mask], order, 0), placed(hx[g, mask], order, bit)], axis=1)
+        y = jnp.dot(x, wide[g][...], preferred_element_type=f32)
         tot[g][mask] = y[0 : tok // 2]
         snd[g][mask, tok // 2 : tok] = y[tok // 2 :].astype(bf16)
         push(at, 0)
 
     def later_step(at, step):
         mask, g = items[at]
-        lo, width, order = groups[g]
+        lo, width, bit, steps = groups[g]
         size = tok >> step
         moving[at, step - 1].wait_recv()
         y = tot[g][mask, 0:size] + rcv[g][mask, size : 2 * size].astype(f32)
-        if step < nb:
+        if step < n_steps:
             half = size // 2
             snd[g][mask, half:size] = y[half:].astype(bf16)
             tot[g][mask, 0:half] = y[:half]
             push(at, step)
-        elif mask == 0:
-            out_ref[ctx, :, lo : lo + width] = y.astype(bf16)
-        else:
-            snd[g][mask, 0:own] = y.astype(bf16)
-            send(
-                snd[g].at[mask, 0:own],
-                out_ref.at[ctx, :, lo : lo + width],
-                out_ssem.at[at],
-                out_rsem.at[at],
-                peer(mask),
-            )
-
+            return
+        snd[g][mask, 0:size] = y.astype(bf16)
+        for side in range(2):
+            if mask == 0 and side == 0:
+                out_ref[ctx, :, kept(g)] = y[0:own].astype(bf16)
+            else:
+                send(
+                    snd[g].at[mask, side * own : (side + 1) * own],
+                    out_ref.at[ctx, :, kept(g)],
+                    out_ssem.at[at, side],
+                    out_rsem.at[at, side],
+                    peer(mask, bit * side),
+                )
+
+    even = [mask for mask in range(2, n_ctx, 2)]
+    for mask in sorted(even, key=lambda k: -low_bit(k)):
+        ho_in[mask].wait_recv()
+        pass_heads(mask)
+    waited = set()
     for at, (mask, g) in enumerate(items):
-        if mask and g == 0:
+        if mask % 2 and mask not in waited:
+            waited.add(mask)
             ho_in[mask].wait_recv()
-            pass_heads(mask)
+        hx_in[g, mask].wait_recv()
+        pass_across(g, mask)
+        if mask == 0:
+            local[3 + g].wait()
+            w_in[g].wait_recv()
         first_step(at)
     lag = n_groups
-    for key in range(len(items) + lag * (nb - 1)):
-        for step in range(1, nb + 1):
+    for key in range(len(items) + lag * (n_steps - 1)):
+        for step in range(1, n_steps + 1):
             at = key - lag * (step - 1)
             if 0 <= at < len(items):
                 later_step(at, step)
 
     for at, (mask, g) in enumerate(items):
-        if mask:
-            lo, width, order = groups[g]
-            pltpu.make_async_remote_copy(
-                src_ref=snd[g].at[mask, 0:own],
-                dst_ref=out_ref.at[flip_all(ctx, mask), :, lo : lo + width],
-                send_sem=out_ssem.at[at],
-                recv_sem=out_rsem.at[at],
-                device_id=peer(mask),
-                device_id_type=MESH,
-            ).wait_recv()
+        lo, width, bit, steps = groups[g]
+        for side in range(2):
+            if mask or side:
+                pltpu.make_async_remote_copy(
+                    src_ref=snd[g].at[mask, side * own : (side + 1) * own],
+                    dst_ref=out_ref.at[flip_all(ctx, mask), :, kept(g, side == 1)],
+                    send_sem=out_ssem.at[at, side],
+                    recv_sem=out_rsem.at[at, side],
+                    device_id=peer(mask, bit * side),
+                    device_id_type=MESH,
+                ).wait_recv()
     for copy in sends:
         copy.wait_send()
 
@@ -333,15 +395,18 @@
         and tok % 128 == 0
         and n_ctx & (n_ctx - 1) == 0
         and n_head & (n_head - 1) == 0
-        and n_head > 1
+        and n_ctx > 1
+        and n_head > 3
+        and width >= 512
     )
     if not full:
         return plain_on_device(q_nope, q_rope, w_uk, w_uv, w_o, cache_kv, new_kv, block_order, cache_lengths)
-    groups = tuple(column_groups(width, bits_of(n_head)))
-    nb = len(bits_of(n_head))
+    groups = column_groups(width, bits_of(n_head))
+    n_groups = len(groups)
+    n_steps = len(bits_of(n_head)) - 1
     dims = (n_ctx, n_head, tok, heads, nope, rope, latent, vdim, slots, groups)
     bf16, f32 = jnp.bfloat16, jnp.float32
-    n_items = n_ctx * len(groups)
+    n_items = n_ctx * n_groups
     dma = pltpu.SemaphoreType.DMA
     vmem = pl.BlockSpec(memory_space=pltpu.VMEM)
     smem = pl.BlockSpec(memory_space=pltpu.SMEM)
@@ -351,21 +416,26 @@
         pltpu.VMEM((n_ctx, latent + rope, slots + tok), bf16),
         pltpu.VMEM((heads * tok, latent), f32),
         pltpu.VMEM((n_ctx, tok, heads * vdim), bf16),
+        pltpu.VMEM((n_groups, n_ctx, tok, heads * vdim), bf16),
         pltpu.VMEM(w_uv.shape, bf16),
-        pltpu.VMEM(w_o.shape, bf16),
     ]
+    scratch += [pltpu.VMEM((2 * depth, g[1]), bf16) for g in groups]
     scratch += [pltpu.VMEM((n_ctx, tok, g[1]), bf16) for g in groups] * 2
     scratch += [pltpu.VMEM((n_ctx, tok // 2, g[1]), f32) for g in groups]
     scratch += [
-        dma((4,)),
+        dma((3 + n_groups,)),
         dma((n_ctx, 2)),
         dma((n_ctx, 2)),
         dma((n_ctx,)),
         dma((n_ctx,)),
-        dma((n_items, nb)),
-        dma((n_items, nb)),
-        dma((n_items,)),
-        dma((n_items,)),
+        dma((n_groups, n_ctx)),
+        dma((n_groups, n_ctx)),
+        dma((n_groups,)),
+        dma((n_groups,)),
+        dma((n_items, n_steps)),
+        dma((n_items, n_steps)),
+        dma((n_items, 2)),
+        dma((n_items, 2)),
     ]
     out = pl.pallas_call(
         functools.partial(kernel, dims),

time: 51.7 us -> 47.9 us (0.926)
  Pallas kernels: 49.9 us -> 46.1 us
    pallas_call x1, Pallas kernels: 49.9 us -> 46.1 us  [on_device(): pl.pallas_call(functools.partial(kernel, dims), out_shape=jax.ShapeDtypeS...]
where the time goes in v2:
time: 47.9 us; the launch traced here: 47.7 us
  Pallas kernels  46.1 us (96%)
  local copies, waits for them, and re-layouts  1.64 us (3%)
    pallas_call x1, Pallas kernels, on_device(): pl.pallas_call(functools.partial(kernel, dims), out_shape=jax.ShapeDtypeS...  46.1 us
    reshape x1, local copies, waits for them, and re-layouts, on_device(): return out.transpose(1, 0, 2).reshape(own, n_ctx * width)  1.64 us

profile of v2, /device:TPU:1, one launch (start us, length us, event | category | flops | bytes accessed | tf_op | source)
XLA Modules:
  0.0 47.7 jit_solution(8424553582412810657)
XLA Ops:
  0.0 46.1 %shard_map.91 = bf16[4,16,1792]{2,1,0:T(8,128)(2,1)} custom-call(bf16[512,128]{1,0:T(8,128)(2,1)} %bitcast.10, bf16[4,64,128]{2,1,0:T(8,128)(2,1)} %bitcast.11, bf16[4,128,512]{2,1,0:T(8,128)(2,1)} %uk_ref.1, bf16[4,512,128]{2,1,0:T(8,128)(2,1)} %uv_hbm.1, bf16[512,1792]{1,0:T(8,128)(2,1)} %wo_hbm.1, bf16[576,128]{1,0:T(8,128)(2,1)} %bitcast.8, ...), custom_call_target="tpu_custom_call" | custom-call | tf_op jit(solution)/shard_map/pallas_call | solution.py:440
  46.1 1.6 %copy.11 = bf16[4,2,8,1792]{3,2,0,1:T(8,128)(2,1)} copy(bf16[4,2,8,1792]{3,2,1,0:T(8,128)(2,1)} %bitcast.7) | data formatting | bytes 458752 | tf_op jit(solution)/shard_map/reshape | solution.py:460

commit v3 on v2

--- a/solution.py
+++ b/solution.py
@@ -91,7 +91,7 @@
 
 
 def column_groups(width, head_bits):
-    first = (width * 4 // 7) // 256 * 256
+    first = (width * 3 // 7) // 256 * 256
     near, far = head_bits[0], head_bits[1]
     return (
         (0, first // 2, near, tuple(b for b in head_bits if b != near)),
@@ -347,7 +347,9 @@
         ho_in[mask].wait_recv()
         pass_heads(mask)
     waited = set()
-    for at, (mask, g) in enumerate(items):
+
+    def begin(at):
+        mask, g = items[at]
         if mask % 2 and mask not in waited:
             waited.add(mask)
             ho_in[mask].wait_recv()
@@ -357,12 +359,16 @@
             local[3 + g].wait()
             w_in[g].wait_recv()
         first_step(at)
-    lag = n_groups
-    for key in range(len(items) + lag * (n_steps - 1)):
-        for step in range(1, n_steps + 1):
-            at = key - lag * (step - 1)
+
+    lag = 3
+    for key in range(len(items) + lag * n_steps):
+        for step in range(n_steps + 1):
+            at = key - lag * step
             if 0 <= at < len(items):
-                later_step(at, step)
+                if step:
+                    later_step(at, step)
+                else:
+                    begin(at)
 
     for at, (mask, g) in enumerate(items):
         lo, width, bit, steps = groups[g]

time: 47.9 us -> 45.4 us (0.948)
  Pallas kernels: 46.1 us -> 43.5 us
    pallas_call x1, Pallas kernels: 46.1 us -> 43.5 us  [on_device(): pl.pallas_call(functools.partial(kernel, dims), out_shape=jax.ShapeDtypeS...]
where the time goes in v3:
time: 45.4 us; the launch traced here: 45.2 us
  Pallas kernels  43.5 us (96%)
  local copies, waits for them, and re-layouts  1.64 us (4%)
    pallas_call x1, Pallas kernels, on_device(): pl.pallas_call(functools.partial(kernel, dims), out_shape=jax.ShapeDtypeS...  43.5 us
    reshape x1, local copies, waits for them, and re-layouts, on_device(): return out.transpose(1, 0, 2).reshape(own, n_ctx * width)  1.64 us

profile of v3, /device:TPU:1, one launch (start us, length us, event | category | flops | bytes accessed | tf_op | source)
XLA Modules:
  0.0 45.2 jit_solution(12534830459805221326)
XLA Ops:
  0.0 43.5 %shard_map.91 = bf16[4,16,1792]{2,1,0:T(8,128)(2,1)} custom-call(bf16[512,128]{1,0:T(8,128)(2,1)} %bitcast.10, bf16[4,64,128]{2,1,0:T(8,128)(2,1)} %bitcast.11, bf16[4,128,512]{2,1,0:T(8,128)(2,1)} %uk_ref.1, bf16[4,512,128]{2,1,0:T(8,128)(2,1)} %uv_hbm.1, bf16[512,1792]{1,0:T(8,128)(2,1)} %wo_hbm.1, bf16[576,128]{1,0:T(8,128)(2,1)} %bitcast.8, ...), custom_call_target="tpu_custom_call" | custom-call | tf_op jit(solution)/shard_map/pallas_call | solution.py:446
  43.6 1.6 %copy.11 = bf16[4,2,8,1792]{3,2,0,1:T(8,128)(2,1)} copy(bf16[4,2,8,1792]{3,2,1,0:T(8,128)(2,1)} %bitcast.7) | data formatting | bytes 458752 | tf_op jit(solution)/shard_map/reshape | solution.py:466
